TPU v7x, 32 devices: a whole 2x2x4 slice. The times are simulated.
32 devices in a mesh: uly: 2 (over y), blk: 16 (over z, x, core).
Axes of the slice: x: 2, y: 2, z: 4, core: 2. Of those that a mesh axis runs over, the one named last changes fastest.
Arguments:
- query_proj: bfloat16 [48, 384, 3072], P('blk', 'uly'), may hold values from -16 to 16
- key_proj: bfloat16 [48, 384, 3072], P('blk', 'uly'), may hold values from -16 to 16
- value_proj: bfloat16 [48, 384, 3072], P('blk', 'uly'), may hold values from -6 to 6
- query_gain: float32 [128], replicated, may hold values from 0.5 to 8
- key_gain: float32 [128], replicated, may hold values from 0.5 to 8
- neighbours: int32 [48, 9], P('blk'), may hold values from 0 to 47, as said below
- tile_counts: int32 [48], P('blk'), may hold values from 1 to 9, as said below
Outputs:
- attention: bfloat16 [48, 384, 3072], P('blk', 'uly')
Inputs may be any that keep to these rules, and one draw needn't show every extreme that they name: `neighbours`: the first tile_counts[t] entries of row t are distinct tiles; entry 0 is t itself; every entry lies in the slab of tile t or in one of the two slabs beside it, a slab being the tiles with equal index // 3; entries at positions tile_counts[t] and beyond equal t. `tile_counts`: some tile lists 9 tiles.
All inputs are finite; a program needn't handle non-finite values.
Results may differ from a plain program's by a relative error of at most 0.005.
The roundings to bfloat16 on the way count: a program that leaves them out, or rounds other values in their place, can miss the bound.
Values may be sent and summed in bfloat16 or wider, within the bound.
A program may use at most 192 MiB of HBM per device.

v0:
```python
import jax
import jax.numpy as jnp
from jax import lax
from jax.sharding import PartitionSpec as P

HD = 128


def shifted(block, axis, distance):
    devices = range(lax.axis_size(axis))
    route = [(i - distance, i) for i in devices if i - distance in devices]
    return lax.ppermute(block, axis, route)


def for_sending(array):

    def short(part):
        return part.astype(jnp.bfloat16) if part.dtype == jnp.float32 else part

    return jax.tree.map(short, array)


def normalize_heads(values_in, gain_vec):
    widened = values_in.astype(jnp.float32)
    widened = widened.reshape(widened.shape[:-1] + (widened.shape[-1] // HD, HD))
    scaled = (
        widened * lax.rsqrt(jnp.mean(widened * widened, axis=-1, keepdims=True) + 1e-06) * gain_vec
    )
    return scaled.astype(jnp.bfloat16).reshape(values_in.shape)


def attend_tile(query_tile, key_tiles, value_tiles, live_count):
    head_count = query_tile.shape[-1] // HD
    inv_root = HD ** (-0.5)
    key_rows = key_tiles.reshape(-1, key_tiles.shape[-1])
    value_rows = value_tiles.reshape(-1, value_tiles.shape[-1])
    live_keys = jnp.repeat(
        jnp.arange(key_tiles.shape[0], dtype=jnp.int32) < live_count, key_tiles.shape[1]
    )
    results = []
    for head in range(head_count):
        query_head = query_tile[:, head * HD : (head + 1) * HD]
        key_head = key_rows[:, head * HD : (head + 1) * HD]
        value_head = value_rows[:, head * HD : (head + 1) * HD]
        scores = (
            lax.dot_general(
                query_head, key_head, (((1,), (1,)), ((), ())), preferred_element_type=jnp.float32
            )
            * inv_root
        )
        scores = jnp.where(live_keys, scores, jnp.float32(-1e30))
        row_max = jnp.max(scores, axis=-1, keepdims=True)
        weights = jnp.where(live_keys, jnp.exp(scores - row_max), jnp.float32(0.0))
        totals = jnp.sum(weights, axis=-1, keepdims=True)
        rounded = weights.astype(jnp.bfloat16)
        numerator = jnp.dot(rounded, value_head, preferred_element_type=jnp.float32)
        results.append((numerator / totals).astype(jnp.bfloat16))
    return jnp.concatenate(results, axis=-1)


def body(query_proj, key_proj, value_proj, query_gain, key_gain, neighbours, tile_counts):
    tiles_here = neighbours.shape[0]
    query_heads, key_heads, value_heads = (
        lax.all_to_all(query_proj, "uly", split_axis=2, concat_axis=1, tiled=True),
        lax.all_to_all(key_proj, "uly", split_axis=2, concat_axis=1, tiled=True),
        lax.all_to_all(value_proj, "uly", split_axis=2, concat_axis=1, tiled=True),
    )
    key_normed = normalize_heads(key_heads, key_gain)
    key_before, value_before = shifted((key_normed, value_heads), "blk", 1)
    key_after, value_after = shifted((key_normed, value_heads), "blk", -1)
    key_window = jnp.concatenate([key_before, key_normed, key_after], axis=0)
    value_window = jnp.concatenate([value_before, value_heads, value_after], axis=0)
    query_norm = normalize_heads(query_heads, query_gain)
    first_tile = (lax.axis_index("blk") - 1) * tiles_here

    def attend(inputs):
        query_tile, slots, live_count = inputs
        local_ids = slots - first_tile
        return attend_tile(query_tile, key_window[local_ids], value_window[local_ids], live_count)

    attended = lax.map(attend, (query_norm, neighbours, tile_counts))
    return jax.tree.map(
        lambda part, own: part.astype(own.dtype),
        lax.all_to_all(for_sending(attended), "uly", split_axis=1, concat_axis=2, tiled=True),
        attended,
    )


def solution(mesh):
    in_specs = (
        P("blk", "uly", None),
        P("blk", "uly", None),
        P("blk", "uly", None),
        P(),
        P(),
        P("blk", None),
        P("blk"),
    )
    out_specs = P("blk", "uly", None)
    return jax.shard_map(body, mesh=mesh, in_specs=in_specs, out_specs=out_specs, check_vma=False)
```

profile of v0, /device:TPU:17, one launch (start us, length us, event | category | flops | bytes accessed | tf_op | source)
XLA Modules:
  0.0 777.6 jit_solution(428730571899325478)
XLA Ops:
  0.0 9.8 %copy.59 = bf16[3,192,3072]{1,0,2:T(4,128)(2,1)} copy(bf16[3,192,3072]{2,1,0:T(8,128)(2,1)} %param.10) | data formatting | bytes 7077888 | tf_op args[1]
  23.4 62.3 %all-to-all-done.1 = bf16[3,192,3072]{1,0,2:T(4,128)(2,1)} async-done(((bf16[3,192,3072]{1,0,2:T(4,128)(2,1)}), bf16[3,192,3072]{1,0,2:T(4,128)(2,1)}, u32[]{:S(2)}, u32[]{:S(2)}) %all-to-all-start.1) | async-done | bytes 3538976 | tf_op jit(solution)/shard_map/all_to_all | solution.py:65
  99.1 8.8 %convert_multiply_fusion = f32[3,192,3072]{1,0,2:T(4,128)} fusion(bf16[3,192,3072]{1,0,2:T(4,128)(2,1)} %all-to-all-done.1), kind=kLoop, calls=%fused_computation.211 | loop fusion | flops 3538944 | bytes 10616832 | tf_op jit(solution)/shard_map/mul | solution.py:27
  107.9 12.2 %copy.62 = f32[3,192,2,1536]{3,1,2,0:T(8,128)} copy(f32[3,192,2,1536]{1,0,3,2:T(4,128)} %bitcast.106) | data formatting | bytes 14155776 | tf_op jit(solution)/shard_map/mul | solution.py:27
  120.1 9.1 %mul.126 = f32[3,384,12,128]{3,2,1,0:T(8,128)} reshape(f32[3,2,192,1536]{3,2,1,0:T(8,128)} %bitcast.112) | data formatting | bytes 14155776 | tf_op jit(solution)/shard_map/mul | solution.py:27
  139.0 8.1 %copy.64 = f32[3,384,1536]{2,1,0:T(8,128)} copy(f32[3,384,1536]{1,2,0:T(8,128)} %bitcast.113) | data formatting | bytes 14155776 | tf_op jit(solution)/shard_map/mul | solution.py:27
  147.1 16.7 %copy.71 = f32[3,192,2,1536]{3,2,1,0:T(2,128)} copy(bf16[3,192,2,1536]{1,0,3,2:T(4,128)(2,1)} %bitcast.53) | data formatting | bytes 10616832 | tf_op jit(solution)/shard_map/convert_element_type | solution.py:24
  163.8 7.2 copy.61
  177.3 8.6 %fusion.256 = bf16[3,384,1536]{2,1,0:T(8,128)(2,1)} fusion(f32[3,384,1536]{2,1,0:T(8,128)} %copy.64, f32[3,2,192,1536]{3,2,1,0:T(8,128)} %copy.61, f32[1536]{0:T(1024)S(1)} %broadcast_bitcast_fusion), kind=kLoop, calls=%fused_computation.207 | loop fusion | flops 5308416 | bytes 17700864 | tf_op jit(solution)/shard_map/convert_element_type | solution.py:29
  192.4 9.8 %copy.66 = bf16[3,2,192,1536]{3,2,1,0:T(8,128)(2,1)} copy(bf16[3,2,192,1536]{2,0,3,1:T(4,128)(2,1)} %bitcast.22) | data formatting | bytes 7077888 | tf_op jit(solution)/shard_map/all_to_all | solution.py:66
  208.1 37.5 %all-to-all-done = bf16[3,192,3072]{1,0,2:T(4,128)(2,1)} async-done(((bf16[3,192,3072]{1,0,2:T(4,128)(2,1)}), bf16[3,192,3072]{1,0,2:T(4,128)(2,1)}, u32[]{:S(2)}, u32[]{:S(2)}) %all-to-all-start) | async-done | bytes 3538976 | tf_op jit(solution)/shard_map/all_to_all | solution.py:64
  245.6 8.8 %convert_multiply_fusion.1 = f32[3,192,3072]{1,0,2:T(4,128)} fusion(bf16[3,192,3072]{1,0,2:T(4,128)(2,1)} %all-to-all-done), kind=kLoop, calls=%fused_computation.212 | loop fusion | flops 3538944 | bytes 10616832 | tf_op jit(solution)/shard_map/mul | solution.py:27
  254.4 12.2 %copy.56 = f32[3,192,2,1536]{3,1,2,0:T(8,128)} copy(f32[3,192,2,1536]{1,0,3,2:T(4,128)} %bitcast.107) | data formatting | bytes 14155776 | tf_op jit(solution)/shard_map/mul | solution.py:27
  266.6 9.1 %mul.114 = f32[3,384,12,128]{3,2,1,0:T(8,128)} reshape(f32[3,2,192,1536]{3,2,1,0:T(8,128)} %bitcast.114) | data formatting | bytes 14155776 | tf_op jit(solution)/shard_map/mul | solution.py:27
  285.5 8.1 %copy.58 = f32[3,384,1536]{2,1,0:T(8,128)} copy(f32[3,384,1536]{1,2,0:T(8,128)} %bitcast.115) | data formatting | bytes 14155776 | tf_op jit(solution)/shard_map/mul | solution.py:27
  293.6 16.8 %copy.70 = f32[3,192,2,1536]{3,2,1,0:T(2,128)} copy(bf16[3,192,2,1536]{1,0,3,2:T(4,128)(2,1)} %bitcast.52) | data formatting | bytes 10616832 | tf_op jit(solution)/shard_map/convert_element_type | solution.py:24
  310.4 7.4 copy.55
  324.5 9.4 %pad_maximum_fusion = bf16[9,384,1536]{2,1,0:T(8,128)(2,1)} fusion(bf16[3,384,1536]{2,1,0:T(8,128)(2,1)} %collective-permute-done.1, bf16[3,384,1536]{2,1,0:T(8,128)(2,1)} %fusion.256, bf16[3,384,1536]{2,1,0:T(8,128)(2,1)} %collective-permute-done), kind=kLoop, calls=%fused_computation.203 | loop fusion | flops 10616832 | bytes 21233664 | tf_op jit(solution)/shard_map/concatenate | solution.py:71
  333.8 9.8 %collective-permute-done.3 = bf16[3,384,1536]{2,1,0:T(8,128)(2,1)} collective-permute-done((bf16[3,384,1536]{2,1,0:T(8,128)(2,1)}, bf16[3,384,1536]{2,1,0:T(8,128)(2,1)}, u32[]{:S(2)}, u32[]{:S(2)}) %collective-permute-start.3) | collective-permute-done | bytes 3538976 | tf_op jit(solution)/shard_map/ppermute | solution.py:12
  343.6 9.4 %pad_maximum_fusion.1 = bf16[9,384,1536]{2,1,0:T(8,128)(2,1)} fusion(bf16[3,384,1536]{2,1,0:T(8,128)(2,1)} %collective-permute-done.3, bf16[3,384,1536]{2,1,0:T(8,128)(2,1)} %bitcast.23, bf16[3,384,1536]{2,1,0:T(8,128)(2,1)} %collective-permute-done.2), kind=kLoop, calls=%fused_computation.204 | loop fusion | flops 10616832 | bytes 21233664 | tf_op jit(solution)/shard_map/concatenate | solution.py:72
  353.0 361.9 %while.10 = (s32[]{:T(128)}, bf16[3,384,1536]{1,2,0:T(8,128)(2,1)}, s32[3]{0:T(128)S(1)}, bf16[3,384,1536]{2,1,0:T(8,128)(2,1)}, s32[3,9]{1,0:T(4,128)}, /*index...) while((s32[]{:T(128)}, bf16[3,384,1536]{1,2,0:T(8,128)(2,1)}, ...), condition=%wide.region_27.28_spmd, body=%wide.region_2.27_spmd.sunk | while | flops 8298225152 | bytes 373581760 | solution.py:81
  375.0 9.5 %gather_fusion = bf16[9,384,1536]{2,1,0:T(8,128)(2,1)} fusion(bf16[9,384,1536]{2,1,0:T(8,128)(2,1)} %get-tuple-element.253, s32[1024]{0:T(1024)S(1)} %pad_clamp_fusion.2), kind=kCustom, calls=%fused_computation.clone.1 | custom fusion | bytes 21233700 | tf_op jit(solution)/shard_map/while/body/eval_jaxpr/gather | solution.py:79
  391.8 9.6 %gather_fusion.1 = bf16[9,384,1536]{2,1,0:T(8,128)(2,1)} fusion(bf16[9,384,1536]{2,1,0:T(8,128)(2,1)} %get-tuple-element.254, s32[1024]{0:T(1024)S(1)} %pad_clamp_fusion.2), kind=kCustom, calls=%fused_computation.1.clone.1 | custom fusion | bytes 21233700 | tf_op jit(solution)/shard_map/while/body/eval_jaxpr/gather | solution.py:79
  430.6 16.4 %fusion.356 = (f32[384]{0:T(512)S(1)}, f32[384]{0:T(512)S(1)}, f32[384]{0:T(512)S(1)}, f32[384]{0:T(512)S(1)}, f32[384]{0:T(512)S(1)}, /*index=5*/f32[384]{0:T(5...) fusion(f32[384,3456]{1,0:T(8,128)S(1)} %get-tuple-element.195, f32[384]{0:T(512)S(1)} %get-tuple-element.196, ...), kind=kLoop, calls=%fused_computation.60.clone.1 | loop fusion | flops 35828352 | bytes 47806848 | tf_op jit(solution)/shard_map/while/body/eval_jaxpr/reduce_sum | solution.py:54
  488.5 9.5 %gather_fusion = bf16[9,384,1536]{2,1,0:T(8,128)(2,1)} fusion(bf16[9,384,1536]{2,1,0:T(8,128)(2,1)} %get-tuple-element.253, s32[1024]{0:T(1024)S(1)} %pad_clamp_fusion.2), kind=kCustom, calls=%fused_computation.clone.1 | custom fusion | bytes 21233700 | tf_op jit(solution)/shard_map/while/body/eval_jaxpr/gather | solution.py:79
  505.4 9.6 %gather_fusion.1 = bf16[9,384,1536]{2,1,0:T(8,128)(2,1)} fusion(bf16[9,384,1536]{2,1,0:T(8,128)(2,1)} %get-tuple-element.254, s32[1024]{0:T(1024)S(1)} %pad_clamp_fusion.2), kind=kCustom, calls=%fused_computation.1.clone.1 | custom fusion | bytes 21233700 | tf_op jit(solution)/shard_map/while/body/eval_jaxpr/gather | solution.py:79
  544.1 16.4 %fusion.356 = (f32[384]{0:T(512)S(1)}, f32[384]{0:T(512)S(1)}, f32[384]{0:T(512)S(1)}, f32[384]{0:T(512)S(1)}, f32[384]{0:T(512)S(1)}, /*index=5*/f32[384]{0:T(5...) fusion(f32[384,3456]{1,0:T(8,128)S(1)} %get-tuple-element.195, f32[384]{0:T(512)S(1)} %get-tuple-element.196, ...), kind=kLoop, calls=%fused_computation.60.clone.1 | loop fusion | flops 35828352 | bytes 47806848 | tf_op jit(solution)/shard_map/while/body/eval_jaxpr/reduce_sum | solution.py:54
  602.1 9.5 %gather_fusion = bf16[9,384,1536]{2,1,0:T(8,128)(2,1)} fusion(bf16[9,384,1536]{2,1,0:T(8,128)(2,1)} %get-tuple-element.253, s32[1024]{0:T(1024)S(1)} %pad_clamp_fusion.2), kind=kCustom, calls=%fused_computation.clone.1 | custom fusion | bytes 21233700 | tf_op jit(solution)/shard_map/while/body/eval_jaxpr/gather | solution.py:79
  618.9 9.6 %gather_fusion.1 = bf16[9,384,1536]{2,1,0:T(8,128)(2,1)} fusion(bf16[9,384,1536]{2,1,0:T(8,128)(2,1)} %get-tuple-element.254, s32[1024]{0:T(1024)S(1)} %pad_clamp_fusion.2), kind=kCustom, calls=%fused_computation.1.clone.1 | custom fusion | bytes 21233700 | tf_op jit(solution)/shard_map/while/body/eval_jaxpr/gather | solution.py:79
  657.6 16.4 %fusion.356 = (f32[384]{0:T(512)S(1)}, f32[384]{0:T(512)S(1)}, f32[384]{0:T(512)S(1)}, f32[384]{0:T(512)S(1)}, f32[384]{0:T(512)S(1)}, /*index=5*/f32[384]{0:T(5...) fusion(f32[384,3456]{1,0:T(8,128)S(1)} %get-tuple-element.195, f32[384]{0:T(512)S(1)} %get-tuple-element.196, ...), kind=kLoop, calls=%fused_computation.60.clone.1 | loop fusion | flops 35828352 | bytes 47806848 | tf_op jit(solution)/shard_map/while/body/eval_jaxpr/reduce_sum | solution.py:54
  714.9 8.7 %copy.67 = bf16[3,384,1536]{2,0,1:T(4,128)(2,1)} copy(bf16[3,384,1536]{1,2,0:T(8,128)(2,1)} %get-tuple-element.47) | data formatting | bytes 7077888 | tf_op jit(solution)/shard_map/while | solution.py:81
  723.6 50.5 %all_to_all.54 = bf16[3,384,1536]{2,0,1:T(4,128)(2,1)S(1)} all-to-all(bf16[3,384,1536]{2,0,1:T(4,128)(2,1)} %copy.67), channel_id=1, replica_groups=mesh['uly'=2,'blk'=16] {'uly'}, dimensions={1} | all-to-all | bytes 7077888 | tf_op jit(solution)/shard_map/all_to_all | solution.py:84
  (239 shorter events, 308.3 us)
Async XLA Ops:
  0.0 99.1 %copy-start = (f32[128]{0:T(128)S(1)}, f32[128]{0:T(128)}, u32[]{:S(2)}) copy-start(f32[128]{0:T(128)} %param.13) | copy-start | bytes 1540
  9.8 75.8 %all-to-all-start.1 = ((bf16[3,192,3072]{1,0,2:T(4,128)(2,1)}), bf16[3,192,3072]{1,0,2:T(4,128)(2,1)}, u32[]{:S(2)}, u32[]{:S(2)}) async-start(bf16[3,192,3072]{1,0,2:T(4,128)(2,1)} %copy.59), calls=%async_computation.1 | async-start | bytes 12582912 | tf_op jit(solution)/shard_map/all_to_all | solution.py:65
  23.4 68.7 %copy-start.3 = (bf16[3,192,3072]{2,1,0:T(8,128)(2,1)S(1)}, bf16[3,192,3072]{2,1,0:T(8,128)(2,1)}, u32[]{:S(2)}) copy-start(bf16[3,192,3072]{2,1,0:T(8,128)(2,1)} %param.9) | copy-start | bytes 10616836
  85.7 85.3 %all-to-all-start.2 = ((bf16[3,192,3072]{1,0,2:T(4,128)(2,1)}), bf16[3,192,3072]{1,0,2:T(4,128)(2,1)}, u32[]{:S(2)}, u32[]{:S(2)}) async-start(bf16[3,192,3072]{1,0,2:T(4,128)(2,1)} %copy.65), calls=%async_computation.2 | async-start | bytes 12582912 | tf_op jit(solution)/shard_map/all_to_all | solution.py:66
  171.0 74.6 %all-to-all-start = ((bf16[3,192,3072]{1,0,2:T(4,128)(2,1)}), bf16[3,192,3072]{1,0,2:T(4,128)(2,1)}, u32[]{:S(2)}, u32[]{:S(2)}) async-start(bf16[3,192,3072]{1,0,2:T(4,128)(2,1)} %copy.53), calls=%async_computation | async-start | bytes 12582912 | tf_op jit(solution)/shard_map/all_to_all | solution.py:64
  177.2 15.1 %copy-start.4 = (f32[128]{0:T(128)S(1)}, f32[128]{0:T(128)}, u32[]{:S(2)}) copy-start(f32[128]{0:T(128)} %param.12) | copy-start | bytes 1540
  185.9 138.6 %collective-permute-start.1 = (bf16[3,384,1536]{2,1,0:T(8,128)(2,1)}, bf16[3,384,1536]{2,1,0:T(8,128)(2,1)}, u32[]{:S(2)}, u32[]{:S(2)}) collective-permute-start(bf16[3,384,1536]{2,1,0:T(8,128)(2,1)} %fusion.256), channel_id=1, source_target_pairs={{1,0},{2,1},{3,2},{4,3},{5,4},{6,5},{7,6},{8,7},{9,8},{10,9},{11,1... | collective-permute-start | bytes 10616840 | tf_op jit(solution)/shard_map/ppermute | solution.py:12
  189.3 135.2 %collective-permute-start = (bf16[3,384,1536]{2,1,0:T(8,128)(2,1)}, bf16[3,384,1536]{2,1,0:T(8,128)(2,1)}, u32[]{:S(2)}, u32[]{:S(2)}) collective-permute-start(bf16[3,384,1536]{2,1,0:T(8,128)(2,1)} %fusion.256), channel_id=1, source_target_pairs={{0,1},{1,2},{2,3},{3,4},{4,5},{5,6},{6,7},{7,8},{8,9},{9,10},{10,1... | collective-permute-start | bytes 10616840 | tf_op jit(solution)/shard_map/ppermute | solution.py:12
  202.2 141.4 %collective-permute-start.3 = (bf16[3,384,1536]{2,1,0:T(8,128)(2,1)}, bf16[3,384,1536]{2,1,0:T(8,128)(2,1)}, u32[]{:S(2)}, u32[]{:S(2)}) collective-permute-start(bf16[3,384,1536]{2,1,0:T(8,128)(2,1)} %bitcast.23), channel_id=1, source_target_pairs={{1,0},{2,1},{3,2},{4,3},{5,4},{6,5},{7,6},{8,7},{9,8},{10,9},{11,1... | collective-permute-start | bytes 10616840 | tf_op jit(solution)/shard_map/ppermute | solution.py:12
  204.1 139.5 %collective-permute-start.2 = (bf16[3,384,1536]{2,1,0:T(8,128)(2,1)}, bf16[3,384,1536]{2,1,0:T(8,128)(2,1)}, u32[]{:S(2)}, u32[]{:S(2)}) collective-permute-start(bf16[3,384,1536]{2,1,0:T(8,128)(2,1)} %bitcast.23), channel_id=1, source_target_pairs={{0,1},{1,2},{2,3},{3,4},{4,5},{5,6},{6,7},{7,8},{8,9},{9,10},{10,1... | collective-permute-start | bytes 10616840 | tf_op jit(solution)/shard_map/ppermute | solution.py:12
  293.6 24.2 %slice-start.13 = ((s8[7077888]{0:T(1024)(128)(4,1)}), s8[2883584]{0:T(1024)(128)(4,1)S(1)}, s32[]{:S(2)}) async-start(s8[7077888]{0:T(1024)(128)(4,1)} %bitcast.110), calls=%async_computation.17 | async-start | bytes 5767168
  333.8 19.2 %copy-start.5 = (s32[3]{0:T(128)S(1)}, s32[3]{0:T(128)}, u32[]{:S(2)}) copy-start(s32[3]{0:T(128)} %param.15) | copy-start | bytes 40
  401.4 15.9 %slice-start = ((s8[10616832]{0:T(1024)(128)(4,1)}), s8[4194304]{0:T(1024)(128)(4,1)S(1)}, s32[]{:S(2)}) async-start(s8[10616832]{0:T(1024)(128)(4,1)} %bitcast.75), calls=%async_computation.4 | async-start | bytes 8388608 | tf_op jit(solution)/shard_map/while
  403.8 13.5 %slice-start.1 = ((s8[10616832]{0:T(1024)(128)(4,1)}), s8[4194304]{0:T(1024)(128)(4,1)S(1)}, s32[]{:S(2)}) async-start(s8[10616832]{0:T(1024)(128)(4,1)} %bitcast.75), calls=%async_computation.5 | async-start | bytes 8388608 | tf_op jit(solution)/shard_map/while
  408.3 9.0 %slice-start.2 = ((s8[10616832]{0:T(1024)(128)(4,1)}), s8[2228224]{0:T(1024)(128)(4,1)S(1)}, s32[]{:S(2)}) async-start(s8[10616832]{0:T(1024)(128)(4,1)} %bitcast.75), calls=%async_computation.6 | async-start | bytes 4456448 | tf_op jit(solution)/shard_map/while
  447.0 12.0 %slice-start.11 = ((s8[5308416]{0:T(1024)(128)(4,1)}), s8[4194304]{0:T(1024)(128)(4,1)S(1)}, s32[]{:S(2)}) async-start(s8[5308416]{0:T(1024)(128)(4,1)} %bitcast.92), calls=%async_computation.15 | async-start | bytes 8388608 | tf_op jit(solution)/shard_map/while
  451.0 8.0 %slice-start.12 = ((s8[5308416]{0:T(1024)(128)(4,1)}), s8[1114112]{0:T(1024)(128)(4,1)S(1)}, s32[]{:S(2)}) async-start(s8[5308416]{0:T(1024)(128)(4,1)} %bitcast.92), calls=%async_computation.16 | async-start | bytes 2228224 | tf_op jit(solution)/shard_map/while
  451.0 10.5 %slice-start.9 = ((s8[5308416]{0:T(1024)(128)(4,1)}), s8[4194304]{0:T(1024)(128)(4,1)S(1)}, s32[]{:S(2)}) async-start(s8[5308416]{0:T(1024)(128)(4,1)} %bitcast.90), calls=%async_computation.13 | async-start | bytes 8388608 | tf_op jit(solution)/shard_map/while
  455.0 8.9 %slice-start.7 = ((s8[5308416]{0:T(1024)(128)(4,1)}), s8[4194304]{0:T(1024)(128)(4,1)S(1)}, s32[]{:S(2)}) async-start(s8[5308416]{0:T(1024)(128)(4,1)} %bitcast.88), calls=%async_computation.11 | async-start | bytes 8388608 | tf_op jit(solution)/shard_map/while
  515.0 15.9 %slice-start = ((s8[10616832]{0:T(1024)(128)(4,1)}), s8[4194304]{0:T(1024)(128)(4,1)S(1)}, s32[]{:S(2)}) async-start(s8[10616832]{0:T(1024)(128)(4,1)} %bitcast.75), calls=%async_computation.4 | async-start | bytes 8388608 | tf_op jit(solution)/shard_map/while
  517.3 13.5 %slice-start.1 = ((s8[10616832]{0:T(1024)(128)(4,1)}), s8[4194304]{0:T(1024)(128)(4,1)S(1)}, s32[]{:S(2)}) async-start(s8[10616832]{0:T(1024)(128)(4,1)} %bitcast.75), calls=%async_computation.5 | async-start | bytes 8388608 | tf_op jit(solution)/shard_map/while
  521.9 9.0 %slice-start.2 = ((s8[10616832]{0:T(1024)(128)(4,1)}), s8[2228224]{0:T(1024)(128)(4,1)S(1)}, s32[]{:S(2)}) async-start(s8[10616832]{0:T(1024)(128)(4,1)} %bitcast.75), calls=%async_computation.6 | async-start | bytes 4456448 | tf_op jit(solution)/shard_map/while
  560.5 12.0 %slice-start.11 = ((s8[5308416]{0:T(1024)(128)(4,1)}), s8[4194304]{0:T(1024)(128)(4,1)S(1)}, s32[]{:S(2)}) async-start(s8[5308416]{0:T(1024)(128)(4,1)} %bitcast.92), calls=%async_computation.15 | async-start | bytes 8388608 | tf_op jit(solution)/shard_map/while
  564.5 8.0 %slice-start.12 = ((s8[5308416]{0:T(1024)(128)(4,1)}), s8[1114112]{0:T(1024)(128)(4,1)S(1)}, s32[]{:S(2)}) async-start(s8[5308416]{0:T(1024)(128)(4,1)} %bitcast.92), calls=%async_computation.16 | async-start | bytes 2228224 | tf_op jit(solution)/shard_map/while
  564.5 10.5 %slice-start.9 = ((s8[5308416]{0:T(1024)(128)(4,1)}), s8[4194304]{0:T(1024)(128)(4,1)S(1)}, s32[]{:S(2)}) async-start(s8[5308416]{0:T(1024)(128)(4,1)} %bitcast.90), calls=%async_computation.13 | async-start | bytes 8388608 | tf_op jit(solution)/shard_map/while
  568.5 8.9 %slice-start.7 = ((s8[5308416]{0:T(1024)(128)(4,1)}), s8[4194304]{0:T(1024)(128)(4,1)S(1)}, s32[]{:S(2)}) async-start(s8[5308416]{0:T(1024)(128)(4,1)} %bitcast.88), calls=%async_computation.11 | async-start | bytes 8388608 | tf_op jit(solution)/shard_map/while
  628.5 15.9 %slice-start = ((s8[10616832]{0:T(1024)(128)(4,1)}), s8[4194304]{0:T(1024)(128)(4,1)S(1)}, s32[]{:S(2)}) async-start(s8[10616832]{0:T(1024)(128)(4,1)} %bitcast.75), calls=%async_computation.4 | async-start | bytes 8388608 | tf_op jit(solution)/shard_map/while
  630.9 13.5 %slice-start.1 = ((s8[10616832]{0:T(1024)(128)(4,1)}), s8[4194304]{0:T(1024)(128)(4,1)S(1)}, s32[]{:S(2)}) async-start(s8[10616832]{0:T(1024)(128)(4,1)} %bitcast.75), calls=%async_computation.5 | async-start | bytes 8388608 | tf_op jit(solution)/shard_map/while
  635.4 9.0 %slice-start.2 = ((s8[10616832]{0:T(1024)(128)(4,1)}), s8[2228224]{0:T(1024)(128)(4,1)S(1)}, s32[]{:S(2)}) async-start(s8[10616832]{0:T(1024)(128)(4,1)} %bitcast.75), calls=%async_computation.6 | async-start | bytes 4456448 | tf_op jit(solution)/shard_map/while
  674.1 12.0 %slice-start.11 = ((s8[5308416]{0:T(1024)(128)(4,1)}), s8[4194304]{0:T(1024)(128)(4,1)S(1)}, s32[]{:S(2)}) async-start(s8[5308416]{0:T(1024)(128)(4,1)} %bitcast.92), calls=%async_computation.15 | async-start | bytes 8388608 | tf_op jit(solution)/shard_map/while
  678.1 10.5 %slice-start.9 = ((s8[5308416]{0:T(1024)(128)(4,1)}), s8[4194304]{0:T(1024)(128)(4,1)S(1)}, s32[]{:S(2)}) async-start(s8[5308416]{0:T(1024)(128)(4,1)} %bitcast.90), calls=%async_computation.13 | async-start | bytes 8388608 | tf_op jit(solution)/shard_map/while
  682.1 8.9 %slice-start.7 = ((s8[5308416]{0:T(1024)(128)(4,1)}), s8[4194304]{0:T(1024)(128)(4,1)S(1)}, s32[]{:S(2)}) async-start(s8[5308416]{0:T(1024)(128)(4,1)} %bitcast.88), calls=%async_computation.11 | async-start | bytes 8388608 | tf_op jit(solution)/shard_map/while
  (22 other events, 118.3 us)
where the time goes:
time: 791 us; the launch traced here: 778 us
  local copies, waits for them, and re-layouts  227 us (29%)
  matrix products  210 us (27%)
  other arithmetic  127 us (16%)
  waiting for transfers between devices  110 us (14%)
  blocking collectives  50.5 us (6%)
  starting transfers between devices  31.5 us (4%)
  loops' own time  22.2 us (3%)
    dot_general x36, matrix products, attend_tile(): lax.dot_general(query_head, key_head, (((1,), (1,)), ((), ())), preferred...  111 us
    dot_general x36, matrix products, attend_tile(): numerator = jnp.dot(rounded, value_head, preferred_element_type=jnp.float32)  99.3 us
    all_to_all x1, waiting for transfers between devices, body(): lax.all_to_all(key_proj, 'uly', split_axis=2, concat_axis=1, tiled=True)  62.3 us
    reduce_sum x6, other arithmetic, attend_tile(): totals = jnp.sum(weights, axis=-1, keepdims=True)  58.4 us
    all_to_all x1, blocking collectives, body(): lax.all_to_all(for_sending(attended), 'uly', split_axis=1, concat_axis=2,...  50.5 us
    convert_element_type x4, local copies, waits for them, and re-layouts, normalize_heads(): widened = values_in.astype(jnp.float32)  48.1 us
    mul x4, local copies, waits for them, and re-layouts, normalize_heads(): widened * widened  42.6 us
    all_to_all x1, waiting for transfers between devices, body(): lax.all_to_all(query_proj, 'uly', split_axis=2, concat_axis=1, tiled=True)  37.5 us
  transfers between devices with their start and end apart: 7, of which 3 were waited for; matrix products, arithmetic and copies ran while one was open for 25% of the time, Pallas kernels for 0%

commit v1 on v0

v1 whole, which is shorter than its diff:
```python
import functools
import math

import jax
import jax.numpy as jnp
from jax import lax
from jax.experimental import pallas as pl
from jax.experimental.pallas import tpu as pltpu
from jax.sharding import PartitionSpec as P

HD = 128
LANES = 128
MESH = pl.DeviceIdType.MESH


def normalize(rows, gain):
    wide = rows.astype(jnp.float32)
    mean = jnp.mean(wide * wide, axis=-1, keepdims=True)
    return (wide * lax.rsqrt(mean + 1e-06) * gain).astype(jnp.bfloat16)


def kernel(
    nu, nb, groups, width,
    neighbours, counts, qgain, kgain, q, k, v,
    out,
    kv, qbuf, obuf, kn, vs, s0, s1,
    y_send, y_recv, x_send, x_recv, o_send, o_recv, local_sem, own_sem,
):
    tiles, rows, _ = q.shape
    tile = rows * nu
    heads = width // HD
    span = 3 * tiles
    u, b = lax.axis_index("uly"), lax.axis_index("blk")
    first_tile = (b - 1) * tiles
    has_prev, has_next = b > 0, b < nb - 1

    def peer(p):
        return lax.rem(u + p, nu)

    def source(p):
        return lax.rem(u + nu - p, nu)

    def cols(owner, g):
        return pl.ds(pl.multiple_of((owner * groups + g) * width, LANES), width)

    def part(owner):
        return pl.ds(pl.multiple_of(owner * rows, 16), rows)

    barrier = pltpu.get_barrier_semaphore()
    for p in range(1, nu):
        pl.semaphore_signal(barrier, inc=1, device_id=(peer(p), b), device_id_type=MESH)

    @pl.when(has_prev)
    def _():
        pl.semaphore_signal(barrier, inc=1, device_id=(u, b - 1), device_id_type=MESH)

    @pl.when(has_next)
    def _():
        pl.semaphore_signal(barrier, inc=1, device_id=(u, b + 1), device_id_type=MESH)

    pl.semaphore_wait(
        barrier, nu - 1 + has_prev.astype(jnp.int32) + has_next.astype(jnp.int32)
    )

    def y_copy(g, p, kind, arriving):
        target = peer(p)
        owner = source(p) if arriving else u
        src = (k, v, q)[kind].at[:, :, cols(target, g)]
        if kind == 2:
            dst = qbuf.at[g, :, part(owner), :]
        else:
            dst = kv.at[g, kind, pl.ds(tiles, tiles), part(owner), :]
        return pltpu.make_async_remote_copy(
            src_ref=src, dst_ref=dst,
            send_sem=y_send.at[g, p - 1, kind], recv_sem=y_recv.at[g, p - 1, kind],
            device_id=(target, b), device_id_type=MESH,
        )

    def own_copy(g, kind):
        src = (k, v, q)[kind].at[:, :, cols(u, g)]
        if kind == 2:
            dst = qbuf.at[g, :, part(u), :]
        else:
            dst = kv.at[g, kind, pl.ds(tiles, tiles), part(u), :]
        return pltpu.make_async_copy(src, dst, local_sem.at[g, kind])

    def x_copy(g, way, p, kind):
        owner = source(p)
        if p == 0:
            src = (k, v)[kind].at[:, :, cols(u, g)]
        else:
            src = kv.at[g, kind, pl.ds(tiles, tiles), part(owner), :]
        dst = kv.at[g, kind, pl.ds(2 * tiles * way, tiles), part(owner), :]
        return pltpu.make_async_remote_copy(
            src_ref=src, dst_ref=dst,
            send_sem=x_send.at[g, way, p, kind], recv_sem=x_recv.at[g, way, p, kind],
            device_id=(u, b + 1 - 2 * way), device_id_type=MESH,
        )

    def o_copy(g, p, arriving):
        target = peer(p)
        owner = source(p) if arriving else u
        return pltpu.make_async_remote_copy(
            src_ref=obuf.at[g, :, part(target), :],
            dst_ref=out.at[:, :, cols(owner, g)],
            send_sem=o_send.at[g, p - 1], recv_sem=o_recv.at[g, p - 1],
            device_id=(target, b), device_id_type=MESH,
        )

    def own_out(g):
        return pltpu.make_async_copy(
            obuf.at[g, :, part(u), :], out.at[:, :, cols(u, g)], own_sem.at[g]
        )

    def start_x(g, p):
        @pl.when(has_next)
        def _():
            for kind in range(2):
                x_copy(g, 0, p, kind).start()

        @pl.when(has_prev)
        def _():
            for kind in range(2):
                x_copy(g, 1, p, kind).start()

    def start_group(g):
        for kind in range(3):
            for p in range(1, nu):
                y_copy(g, p, kind, False).start()
        start_x(g, 0)
        for kind in range(3):
            own_copy(g, kind).start()

    def forward(g):
        for p in range(1, nu):
            for kind in range(2):
                y_copy(g, p, kind, True).wait_recv()
            start_x(g, p)

    def arrive(g):
        for kind in range(3):
            own_copy(g, kind).wait()
        for p in range(1, nu):
            y_copy(g, p, 2, True).wait_recv()

        @pl.when(has_prev)
        def _():
            for p in range(nu):
                for kind in range(2):
                    x_copy(g, 0, p, kind).wait_recv()

        @pl.when(has_next)
        def _():
            for p in range(nu):
                for kind in range(2):
                    x_copy(g, 1, p, kind).wait_recv()

    unit = math.log2(math.e) * HD ** (-0.5)
    block = tile // 2
    strips = tile // LANES

    def attend(g):
        key_gain = kgain[...]
        query_gain = qgain[...]

        def stage(w, carry):
            for h in range(heads):
                at = slice(h * HD, (h + 1) * HD)
                kn[h, w] = normalize(kv[g, 0, w, :, at], key_gain)
                vs[h, w] = kv[g, 1, w, :, at]
            return carry

        lax.fori_loop(0, span, stage, 0)

        def query_tile(t, carry):
            count = counts[t]
            ids = [jnp.clip(neighbours[t, j] - first_tile, 0, span - 1) for j in range(neighbours.shape[1])]
            live = [j < count for j in range(len(ids))]
            items = [(h, r) for h in range(heads) for r in range(2)]
            refs = (s0, s1)
            query = top = None
            previous = None
            for n in range(len(items) + 1):
                if n < len(items):
                    h, r = items[n]
                    query = normalize(
                        qbuf[g, t, r * block : (r + 1) * block, h * HD : (h + 1) * HD], query_gain
                    )
                    peak = jnp.full((block, LANES), -1e30, jnp.float32)
                if previous is not None:
                    ph, pr, shift = previous
                    total = jnp.zeros((block, LANES), jnp.float32)
                    gathered = jnp.zeros((block, HD), jnp.float32)
                for j in range(len(ids)):
                    if n < len(items):
                        score = lax.dot_general(
                            query, kn[h, ids[j]], (((1,), (1,)), ((), ())),
                            preferred_element_type=jnp.float32,
                        )
                        refs[n % 2][j] = score
                        high = score[:, :LANES]
                        for c in range(1, strips):
                            high = jnp.maximum(high, score[:, c * LANES : (c + 1) * LANES])
                        peak = jnp.maximum(peak, jnp.where(live[j], high, -1e30))
                    if previous is not None:
                        here = jnp.where(live[j], shift, 1e30)
                        weight = jnp.exp2(refs[(n - 1) % 2][j] * unit - here)
                        for c in range(strips):
                            total = total + weight[:, c * LANES : (c + 1) * LANES]
                        gathered = gathered + jnp.dot(
                            weight.astype(jnp.bfloat16), vs[ph, ids[j]],
                            preferred_element_type=jnp.float32,
                        )
                if previous is not None:
                    whole = jnp.sum(total, axis=-1, keepdims=True)
                    obuf[g, t, pr * block : (pr + 1) * block, ph * HD : (ph + 1) * HD] = (
                        gathered / whole
                    ).astype(jnp.bfloat16)
                if n < len(items):
                    previous = (h, r, jnp.max(peak, axis=-1, keepdims=True) * unit)
            return carry

        lax.fori_loop(0, tiles, query_tile, 0)

    start_group(0)
    if groups > 1:
        start_group(1)
    forward(0)

    def step(g, carry):
        @pl.when(g + 2 < groups)
        def _():
            start_group(g + 2)

        @pl.when(g + 1 < groups)
        def _():
            forward(g + 1)

        arrive(g)
        attend(g)
        for p in range(1, nu):
            o_copy(g, p, False).start()
        own_out(g).start()
        return carry

    lax.fori_loop(0, groups, step, 0)

    def drain(g, carry):
        for p in range(1, nu):
            for kind in range(3):
                y_copy(g, p, kind, False).wait_send()
            o_copy(g, p, False).wait_send()
            o_copy(g, p, True).wait_recv()
        own_out(g).wait()

        @pl.when(has_next)
        def _():
            for p in range(nu):
                for kind in range(2):
                    x_copy(g, 0, p, kind).wait_send()

        @pl.when(has_prev)
        def _():
            for p in range(nu):
                for kind in range(2):
                    x_copy(g, 1, p, kind).wait_send()

        return carry

    lax.fori_loop(0, groups, drain, 0)


def body(nu, nb, query_proj, key_proj, value_proj, query_gain, key_gain, neighbours, tile_counts):
    tiles, rows, full = query_proj.shape
    tile = rows * nu
    local_heads = full // HD // nu
    heads = 2 if local_heads % 2 == 0 else 1
    groups = local_heads // heads
    width = heads * HD
    span = 3 * tiles
    listed = neighbours.shape[1]
    any_space = pl.BlockSpec(memory_space=pl.ANY)
    smem = pl.BlockSpec(memory_space=pltpu.SMEM)
    vmem = pl.BlockSpec(memory_space=pltpu.VMEM)
    dma = pltpu.SemaphoreType.DMA
    return pl.pallas_call(
        functools.partial(kernel, nu, nb, groups, width),
        out_shape=jax.ShapeDtypeStruct(query_proj.shape, query_proj.dtype),
        in_specs=[smem, smem, vmem, vmem, any_space, any_space, any_space],
        out_specs=any_space,
        scratch_shapes=[
            pltpu.VMEM((groups, 2, span, tile, width), jnp.bfloat16),
            pltpu.VMEM((groups, tiles, tile, width), jnp.bfloat16),
            pltpu.VMEM((groups, tiles, tile, width), jnp.bfloat16),
            pltpu.VMEM((heads, span, tile, HD), jnp.bfloat16),
            pltpu.VMEM((heads, span, tile, HD), jnp.bfloat16),
            pltpu.VMEM((listed, tile // 2, tile), jnp.float32),
            pltpu.VMEM((listed, tile // 2, tile), jnp.float32),
            dma((groups, max(nu - 1, 1), 3)),
            dma((groups, max(nu - 1, 1), 3)),
            dma((groups, 2, nu, 2)),
            dma((groups, 2, nu, 2)),
            dma((groups, max(nu - 1, 1))),
            dma((groups, max(nu - 1, 1))),
            dma((groups, 3)),
            dma((groups,)),
        ],
        compiler_params=pltpu.CompilerParams(
            collective_id=0, has_side_effects=True, vmem_limit_bytes=56 * 1024 * 1024
        ),
        name="tile_attention",
    )(
        neighbours, tile_counts, query_gain.reshape(1, HD), key_gain.reshape(1, HD),
        query_proj, key_proj, value_proj,
    )


def solution(mesh):
    nu, nb = mesh.shape["uly"], mesh.shape["blk"]
    in_specs = (
        P("blk", "uly", None),
        P("blk", "uly", None),
        P("blk", "uly", None),
        P(),
        P(),
        P("blk", None),
        P("blk"),
    )
    return jax.shard_map(
        functools.partial(body, nu, nb), mesh=mesh, in_specs=in_specs,
        out_specs=P("blk", "uly", None), check_vma=False,
    )
```

time: 791 us -> 198 us (0.25)
  the two profiles are of different devices: /device:TPU:17 before, /device:TPU:14 now
where the time goes in v1:
time: 198 us
  Pallas kernels  194 us (98%)
  local copies, waits for them, and re-layouts  4.03 us (2%)
    pallas_call x1, Pallas kernels, body(): pl.pallas_call(functools.partial(kernel, nu, nb, groups, width), out_shap...  194 us
    unnamed x1, local copies, waits for them, and re-layouts  4.03 us

profile of v1, /device:TPU:14, one launch (start us, length us, event | category | flops | bytes accessed | tf_op | source)
XLA Modules:
  0.0 197.6 jit_solution(5655471811320882830)
XLA Ops:
  0.0 193.5 %tile_attention.1 = bf16[3,192,3072]{2,1,0:T(8,128)(2,1)} custom-call(s32[3,9]{1,0:T(4,128)} %neighbours.1, s32[3]{0:T(128)} %counts.1, f32[1,128]{1,0:T(1,128)} %bitcast.2, f32[1,128]{1,0:T(1,128)} %bitcast.3, bf16[3,192,3072]{2,1,0:T(8,128)(2,1)} %q.1, bf16[3,192,3072]{2,1,0:T(8,128)(2,1)} %k.1, bf16[3,192,3072]{2,1,0:T(8,128)(2,1)} %v.1), custom_call_target="tpu_custom_call" | custom-call | tf_op jit(solution)/shard_map/tile_attention/pallas_call | solution.py:286
  193.5 4.0 %copy.9 = bf16[3,192,3072]{2,1,0:T(8,128)(2,1)} copy(bf16[3,192,3072]{2,1,0:T(8,128)(2,1)} %tile_attention.1) | data formatting | bytes 7077888

commit v2 on v1

--- a/solution.py
+++ b/solution.py
@@ -28,7 +28,6 @@
 ):
     tiles, rows, _ = q.shape
     tile = rows * nu
-    heads = width // HD
     span = 3 * tiles
     u, b = lax.axis_index("uly"), lax.axis_index("blk")
     first_tile = (b - 1) * tiles
@@ -159,68 +158,75 @@
     block = tile // 2
     strips = tile // LANES
 
-    def attend(g):
+    def attend(g, before_rest):
         key_gain = kgain[...]
         query_gain = qgain[...]
 
         def stage(w, carry):
-            for h in range(heads):
-                at = slice(h * HD, (h + 1) * HD)
-                kn[h, w] = normalize(kv[g, 0, w, :, at], key_gain)
-                vs[h, w] = kv[g, 1, w, :, at]
+            kn[w] = normalize(kv[g, 0, w], key_gain)
+            vs[w] = kv[g, 1, w]
             return carry
 
         lax.fori_loop(0, span, stage, 0)
 
-        def query_tile(t, carry):
-            count = counts[t]
-            ids = [jnp.clip(neighbours[t, j] - first_tile, 0, span - 1) for j in range(neighbours.shape[1])]
-            live = [j < count for j in range(len(ids))]
-            items = [(h, r) for h in range(heads) for r in range(2)]
-            refs = (s0, s1)
-            query = top = None
-            previous = None
-            for n in range(len(items) + 1):
+        items = [(t, r) for t in range(tiles) for r in range(2)]
+        run_items(g, query_gain, items[:2])
+        before_rest()
+        run_items(g, query_gain, items[2:])
+
+    def run_items(g, query_gain, items):
+        refs = (s0, s1)
+        listed = neighbours.shape[1]
+        chunks = [tuple(range(j, min(j + 2, listed))) for j in range(0, listed, 2)]
+        lists = {}
+        for t in sorted({t for t, _ in items}):
+            ids = [jnp.clip(neighbours[t, j] - first_tile, 0, span - 1) for j in range(listed)]
+            lists[t] = ids, [j < counts[t] for j in range(listed)]
+        previous = None
+        for n in range(len(items) + 1):
+            if n < len(items):
+                t, r = items[n]
+                ids, live = lists[t]
+                query = normalize(qbuf[g, t, r * block : (r + 1) * block, :], query_gain)
+                peak = jnp.full((block, LANES), -1e30, jnp.float32)
+            if previous is not None:
+                pt, pr, shift = previous
+                pids, plive = lists[pt]
+                total = jnp.zeros((block, LANES), jnp.float32)
+                gathered = jnp.zeros((block, HD), jnp.float32)
+            for chunk in chunks:
                 if n < len(items):
-                    h, r = items[n]
-                    query = normalize(
-                        qbuf[g, t, r * block : (r + 1) * block, h * HD : (h + 1) * HD], query_gain
+                    keys = jnp.concatenate([kn[ids[j]] for j in chunk], axis=0)
+                    score = lax.dot_general(
+                        query, keys, (((1,), (1,)), ((), ())), preferred_element_type=jnp.float32
                     )
-                    peak = jnp.full((block, LANES), -1e30, jnp.float32)
+                    for i, j in enumerate(chunk):
+                        mine = score[:, i * tile : (i + 1) * tile]
+                        refs[n % 2][j] = mine
+                        high = mine[:, :LANES]
+                        for c in range(1, strips):
+                            high = jnp.maximum(high, mine[:, c * LANES : (c + 1) * LANES])
+                        peak = jnp.maximum(peak, jnp.where(live[j], high, -1e30))
                 if previous is not None:
-                    ph, pr, shift = previous
-                    total = jnp.zeros((block, LANES), jnp.float32)
-                    gathered = jnp.zeros((block, HD), jnp.float32)
-                for j in range(len(ids)):
-                    if n < len(items):
-                        score = lax.dot_general(
-                            query, kn[h, ids[j]], (((1,), (1,)), ((), ())),
-                            preferred_element_type=jnp.float32,
-                        )
-                        refs[n % 2][j] = score
-                        high = score[:, :LANES]
-                        for c in range(1, strips):
-                            high = jnp.maximum(high, score[:, c * LANES : (c + 1) * LANES])
-                        peak = jnp.maximum(peak, jnp.where(live[j], high, -1e30))
-                    if previous is not None:
-                        here = jnp.where(live[j], shift, 1e30)
+                    rounded = []
+                    for j in chunk:
+                        here = jnp.where(plive[j], shift, 1e30)
                         weight = jnp.exp2(refs[(n - 1) % 2][j] * unit - here)
                         for c in range(strips):
                             total = total + weight[:, c * LANES : (c + 1) * LANES]
-                        gathered = gathered + jnp.dot(
-                            weight.astype(jnp.bfloat16), vs[ph, ids[j]],
-                            preferred_element_type=jnp.float32,
-                        )
-                if previous is not None:
-                    whole = jnp.sum(total, axis=-1, keepdims=True)
-                    obuf[g, t, pr * block : (pr + 1) * block, ph * HD : (ph + 1) * HD] = (
-                        gathered / whole
-                    ).astype(jnp.bfloat16)
-                if n < len(items):
-                    previous = (h, r, jnp.max(peak, axis=-1, keepdims=True) * unit)
-            return carry
-
-        lax.fori_loop(0, tiles, query_tile, 0)
+                        rounded.append(weight.astype(jnp.bfloat16))
+                    gathered = gathered + jnp.dot(
+                        jnp.concatenate(rounded, axis=1),
+                        jnp.concatenate([vs[pids[j]] for j in chunk], axis=0),
+                        preferred_element_type=jnp.float32,
+                    )
+            if previous is not None:
+                whole = jnp.sum(total, axis=-1, keepdims=True)
+                obuf[g, pt, pr * block : (pr + 1) * block, :] = (gathered / whole).astype(
+                    jnp.bfloat16
+                )
+            if n < len(items):
+                previous = (t, r, jnp.max(peak, axis=-1, keepdims=True) * unit)
 
     start_group(0)
     if groups > 1:
@@ -228,16 +234,18 @@
     forward(0)
 
     def step(g, carry):
+        def forward_next():
+            @pl.when(g + 1 < groups)
+            def _():
+                forward(g + 1)
+
+        arrive(g)
+
         @pl.when(g + 2 < groups)
         def _():
             start_group(g + 2)
 
-        @pl.when(g + 1 < groups)
-        def _():
-            forward(g + 1)
-
-        arrive(g)
-        attend(g)
+        attend(g, forward_next)
         for p in range(1, nu):
             o_copy(g, p, False).start()
         own_out(g).start()
@@ -273,10 +281,8 @@
 def body(nu, nb, query_proj, key_proj, value_proj, query_gain, key_gain, neighbours, tile_counts):
     tiles, rows, full = query_proj.shape
     tile = rows * nu
-    local_heads = full // HD // nu
-    heads = 2 if local_heads % 2 == 0 else 1
-    groups = local_heads // heads
-    width = heads * HD
+    groups = full // HD // nu
+    width = HD
     span = 3 * tiles
     listed = neighbours.shape[1]
     any_space = pl.BlockSpec(memory_space=pl.ANY)
@@ -292,8 +298,8 @@
             pltpu.VMEM((groups, 2, span, tile, width), jnp.bfloat16),
             pltpu.VMEM((groups, tiles, tile, width), jnp.bfloat16),
             pltpu.VMEM((groups, tiles, tile, width), jnp.bfloat16),
-            pltpu.VMEM((heads, span, tile, HD), jnp.bfloat16),
-            pltpu.VMEM((heads, span, tile, HD), jnp.bfloat16),
+            pltpu.VMEM((span, tile, HD), jnp.bfloat16),
+            pltpu.VMEM((span, tile, HD), jnp.bfloat16),
             pltpu.VMEM((listed, tile // 2, tile), jnp.float32),
             pltpu.VMEM((listed, tile // 2, tile), jnp.float32),
             dma((groups, max(nu - 1, 1), 3)),

time: 198 us -> 204 us (1.030)
  the two profiles are of different devices: /device:TPU:14 before, /device:TPU:17 now
where the time goes in v2:
time: 204 us
  Pallas kernels  200 us (98%)
  local copies, waits for them, and re-layouts  4.03 us (2%)
    pallas_call x1, Pallas kernels, body(): pl.pallas_call(functools.partial(kernel, nu, nb, groups, width), out_shap...  200 us

profile of v2, /device:TPU:17, one launch (start us, length us, event | category | flops | bytes accessed | tf_op | source)
XLA Modules:
  0.0 203.8 jit_solution(11849872614861792129)
XLA Ops:
  0.0 199.8 %tile_attention.1 = bf16[3,192,3072]{2,1,0:T(8,128)(2,1)} custom-call(s32[3,9]{1,0:T(4,128)} %neighbours.1, s32[3]{0:T(128)} %counts.1, f32[1,128]{1,0:T(1,128)} %bitcast.2, f32[1,128]{1,0:T(1,128)} %bitcast.3, bf16[3,192,3072]{2,1,0:T(8,128)(2,1)} %q.1, bf16[3,192,3072]{2,1,0:T(8,128)(2,1)} %k.1, bf16[3,192,3072]{2,1,0:T(8,128)(2,1)} %v.1), custom_call_target="tpu_custom_call" | custom-call | tf_op jit(solution)/shard_map/tile_attention/pallas_call | solution.py:292
  199.8 4.0 %copy.9 = bf16[3,192,3072]{2,1,0:T(8,128)(2,1)} copy(bf16[3,192,3072]{2,1,0:T(8,128)(2,1)} %tile_attention.1) | data formatting | bytes 7077888

commit v3 on v2

--- a/solution.py
+++ b/solution.py
@@ -122,13 +122,17 @@
             for kind in range(2):
                 x_copy(g, 1, p, kind).start()
 
-    def start_group(g):
+    def start_y(g):
         for kind in range(3):
             for p in range(1, nu):
                 y_copy(g, p, kind, False).start()
-        start_x(g, 0)
         for kind in range(3):
             own_copy(g, kind).start()
+
+    def ahead(act, g):
+        @pl.when(g < groups)
+        def _():
+            act(g)
 
     def forward(g):
         for p in range(1, nu):
@@ -136,29 +140,24 @@
                 y_copy(g, p, kind, True).wait_recv()
             start_x(g, p)
 
-    def arrive(g):
+    def arrive_here(g):
         for kind in range(3):
             own_copy(g, kind).wait()
         for p in range(1, nu):
             y_copy(g, p, 2, True).wait_recv()
 
-        @pl.when(has_prev)
+    def arrive_beside(g, way):
+        @pl.when((has_prev, has_next)[way])
         def _():
             for p in range(nu):
                 for kind in range(2):
-                    x_copy(g, 0, p, kind).wait_recv()
-
-        @pl.when(has_next)
-        def _():
-            for p in range(nu):
-                for kind in range(2):
-                    x_copy(g, 1, p, kind).wait_recv()
+                    x_copy(g, way, p, kind).wait_recv()
 
     unit = math.log2(math.e) * HD ** (-0.5)
     block = tile // 2
     strips = tile // LANES
 
-    def attend(g, before_rest):
+    def attend(g, before_first, before_rest):
         key_gain = kgain[...]
         query_gain = qgain[...]
 
@@ -167,7 +166,12 @@
             vs[w] = kv[g, 1, w]
             return carry
 
-        lax.fori_loop(0, span, stage, 0)
+        arrive_here(g)
+        lax.fori_loop(tiles, 2 * tiles, stage, 0)
+        for way in range(2):
+            arrive_beside(g, way)
+            lax.fori_loop(2 * tiles * way, (2 * way + 1) * tiles, stage, 0)
+        before_first()
 
         items = [(t, r) for t in range(tiles) for r in range(2)]
         run_items(g, query_gain, items[:2])
@@ -228,24 +232,25 @@
             if n < len(items):
                 previous = (t, r, jnp.max(peak, axis=-1, keepdims=True) * unit)
 
-    start_group(0)
-    if groups > 1:
-        start_group(1)
+    for g in range(min(3, groups)):
+        start_y(g)
+        start_x(g, 0)
     forward(0)
+    if groups > 3:
+        start_y(3)
 
     def step(g, carry):
-        def forward_next():
-            @pl.when(g + 1 < groups)
+        def before_first():
+            @pl.when(g == 0)
             def _():
-                forward(g + 1)
-
-        arrive(g)
-
-        @pl.when(g + 2 < groups)
-        def _():
-            start_group(g + 2)
-
-        attend(g, forward_next)
+                ahead(forward, g + 1)
+                ahead(start_y, g + 4)
+                ahead(lambda n: start_x(n, 0), g + 3)
+
+            ahead(start_y, g + 5)
+            ahead(lambda n: start_x(n, 0), g + 4)
+
+        attend(g, before_first, lambda: ahead(forward, g + 2))
         for p in range(1, nu):
             o_copy(g, p, False).start()
         own_out(g).start()

time: 204 us -> 190 us (0.931); the launches traced: 204 us -> 187 us
  Pallas kernels: 200 us -> 183 us
    pallas_call x1, Pallas kernels: 200 us -> 183 us  [body(): pl.pallas_call(functools.partial(kernel, nu, nb, groups, width), out_shap...]
where the time goes in v3:
time: 190 us; the launch traced here: 187 us
  Pallas kernels  183 us (96%)
  local copies, waits for them, and re-layouts  4.03 us (2%)
    pallas_call x1, Pallas kernels, body(): pl.pallas_call(functools.partial(kernel, nu, nb, groups, width), out_shap...  183 us
    unnamed x1, local copies, waits for them, and re-layouts  4.03 us

profile of v3, /device:TPU:17, one launch (start us, length us, event | category | flops | bytes accessed | tf_op | source)
XLA Modules:
  0.0 187.0 jit_solution(15254063061449160656)
XLA Ops:
  0.0 183.0 %tile_attention.1 = bf16[3,192,3072]{2,1,0:T(8,128)(2,1)} custom-call(s32[3,9]{1,0:T(4,128)} %neighbours.1, s32[3]{0:T(128)} %counts.1, f32[1,128]{1,0:T(1,128)} %bitcast.2, f32[1,128]{1,0:T(1,128)} %bitcast.3, bf16[3,192,3072]{2,1,0:T(8,128)(2,1)} %q.1, bf16[3,192,3072]{2,1,0:T(8,128)(2,1)} %k.1, bf16[3,192,3072]{2,1,0:T(8,128)(2,1)} %v.1), custom_call_target="tpu_custom_call" | custom-call | tf_op jit(solution)/shard_map/tile_attention/pallas_call | solution.py:297
  183.0 4.0 %copy.9 = bf16[3,192,3072]{2,1,0:T(8,128)(2,1)} copy(bf16[3,192,3072]{2,1,0:T(8,128)(2,1)} %tile_attention.1) | data formatting | bytes 7077888
